TPU v7x, 512 devices: a whole 4x4x16 slice. The times are simulated.
512 devices in a mesh: atlas: 4 (over y), row: 32 (over z, core), col: 4 (over x).
Axes of the slice: x: 4, y: 4, z: 16, core: 2. Of those that a mesh axis runs over, the one named last changes fastest.
Arguments:
- cells: bfloat16 [4, 64, 16384], P('atlas', None, 'row'), may hold values from -4 to 4
- support: bfloat16 [64, 16384], P(None, 'col'), may hold values from -4 to 4
Outputs:
- cell_dual: float32 [4, 16384], P('atlas', 'row')
- support_dual: float32 [4, 16384], P('atlas', 'col')
- new_support: float32 [64, 16384], P(None, 'col')
All inputs are finite; a program needn't handle non-finite values.
Results may differ from a plain program's by a relative error of at most 0.001.
Values sent between devices are 32-bit elements; how exact they have to be, the bound alone decides.
A program may use at most 64 MiB of HBM per device.

v0:
```python
import jax
import jax.numpy as jnp
from jax import lax
from jax.sharding import Mesh
from jax.sharding import PartitionSpec as P

ITERS = 2
ROW = ("row_0", "row_1")


blur = 0.1


def copy_for_each(x, axis):
    length = lax.axis_size(axis)
    return lax.all_to_all(jnp.broadcast_to(x[None], (length, *x.shape)), axis, 0, 0, tiled=True)


def collected_together(x, axis):
    leaves = jax.tree.leaves(x)
    turns = sorted(range(len(leaves)), key=lambda k: -leaves[k].size)
    width = (1, *leaves[turns[0]].shape)[-1]
    lines = [
        jnp.pad(leaves[k].reshape(-1), (0, -leaves[k].size % width)).reshape(-1, width)
        for k in turns
    ]
    both, at, found = (copy_for_each(jnp.concatenate(lines), axis), 0, {})
    for k, line in zip(turns, lines):
        slab = both[:, at : at + len(line)].reshape(len(both), -1)
        found[k] = slab[:, : leaves[k].size].reshape(-1, *leaves[k].shape)
        at += len(line)
    numbers = iter(range(len(leaves)))
    return jax.tree.map(lambda _: found[next(numbers)], x)


def combined_pairwise(pieces, combine):
    while len(jax.tree.leaves(pieces)[0]) > 1:
        pieces = jax.vmap(combine)(
            *(jax.tree.map(lambda part: part[side::2], pieces) for side in (0, 1))
        )
    return jax.tree.map(lambda part: part[0], pieces)


def merged(x, axis, combine):
    pieces = collected_together(x, axis)
    return combined_pairwise(pieces, combine)


def gathered_once(x, axis):
    leaves = jax.tree.leaves(x)
    turns = sorted(range(len(leaves)), key=lambda k: -leaves[k].size)
    width = (1, *leaves[turns[0]].shape)[-1]
    lines = [
        jnp.pad(leaves[k].reshape(-1), (0, -leaves[k].size % width)).reshape(-1, width)
        for k in turns
    ]
    both, at, found = (lax.all_gather(jnp.concatenate(lines), axis), 0, {})
    for k, line in zip(turns, lines):
        slab = both[:, at : at + len(line)].reshape(len(both), -1)
        found[k] = slab[:, : leaves[k].size].reshape(-1, *leaves[k].shape)
        at += len(line)
    numbers = iter(range(len(leaves)))
    return jax.tree.map(lambda _: found[next(numbers)], x)


def merged_by_axis(x, axes, combine):
    for axis in axes:
        pieces = gathered_once(x, axis)
        x = jax.tree.map(lambda part: part[0], pieces)
        for k in range(1, lax.axis_size(axis)):
            x = combine(x, jax.tree.map(lambda part: part[k], pieces))
    return x


def padded_to(lines, length):
    spare = -len(lines) % length
    return jnp.pad(lines, [(0, spare)] + [(0, 0)] * (lines.ndim - 1))


def joined_along(pieces, dim):
    pieces = jnp.moveaxis(pieces, 0, dim)
    shape = pieces.shape
    return pieces.reshape(*shape[:dim], shape[dim] * shape[dim + 1], *shape[dim + 2 :])


def whole_of(x, axes, dim):
    far, near = axes
    pieces = copy_for_each(copy_for_each(x, far), near)
    return joined_along(pieces.swapaxes(0, 1).reshape(-1, *x.shape), dim)


def in_blocks(x, dim, length):
    shape = x.shape
    pieces = x.reshape(*shape[:dim], length, shape[dim] // length, *shape[dim + 1 :])
    return jnp.moveaxis(pieces, dim, 0)


def sum_at_owner(x, axis, dim):
    length = lax.axis_size(axis)
    pieces = lax.all_to_all(in_blocks(x, dim, length), axis, 0, 0, tiled=True)
    return jnp.sum(pieces, axis=0)


def summed_rows(x, axes, dim):
    far, near = axes
    pieces = in_blocks(x, dim, lax.axis_size(far))
    nearer = sum_at_owner(pieces, near, dim + 1)
    arrived = lax.all_to_all(nearer, far, split_axis=0, concat_axis=0, tiled=True)
    return arrived.sum(axis=0)


def total_of(x, axes):
    lines = x.reshape(-1)
    padded = padded_to(lines, lax.axis_size(axes[0]) * lax.axis_size(axes[1]))
    whole = whole_of(summed_rows(padded, axes, 0), axes, 0)
    return lax.slice_in_dim(whole, 0, len(lines)).reshape(x.shape)


def lse_pair(first, second):
    top_one, total_one = first
    top_two, total_two = second
    peak = jnp.maximum(top_one, top_two)
    return (peak, total_one * jnp.exp(top_one - peak) + total_two * jnp.exp(top_two - peak))


def shards(cells, support):
    points = cells[0]
    dims, rows = points.shape
    columns = support.shape[1]
    width_block = min(512, columns)
    count = columns // width_block
    points_wide = points.astype(jnp.float32)
    squares_x = jnp.sum(jnp.square(points_wide), axis=0)
    squares_y = jnp.sum(jnp.square(support.astype(jnp.float32)), axis=0)
    total_cells = rows * lax.axis_size(ROW)
    total_support = columns * lax.axis_size("col")
    atlases = lax.axis_size("atlas")

    def tile_cost(start):
        piece = lax.dynamic_slice_in_dim(support, start, width_block, 1)
        near = lax.dynamic_slice_in_dim(squares_y, start, width_block, 0)
        cross = lax.dot_general(
            points, piece, (((0,), (0,)), ((), ())), preferred_element_type=jnp.float32
        )
        return (squares_x[:, None] + near[None, :] - 2.0 * cross) / dims

    def row_step(dual_g):

        def row_visit(index, carry):
            top, total = carry
            start = index * width_block
            gpart = lax.dynamic_slice_in_dim(dual_g, start, width_block, 0)
            logits = (gpart[None, :] - tile_cost(start)) / blur
            peak = jnp.maximum(top, jnp.max(logits, axis=1))
            total = total * jnp.exp(top - peak) + jnp.sum(jnp.exp(logits - peak[:, None]), axis=1)
            return (peak, total)

        start_carry = (jnp.full((rows,), -jnp.inf, jnp.float32), jnp.zeros((rows,), jnp.float32))
        top, total = lax.fori_loop(0, count, row_visit, start_carry)
        top, total = merged((top, total), "col", lse_pair)
        return blur * jnp.log(1.0 / total_cells) - blur * (top + jnp.log(total))

    def column_step(dual_f):

        def column_visit(index, carry):
            top, total = carry
            start = index * width_block
            logits = (dual_f[:, None] - tile_cost(start)) / blur
            peak = jnp.max(logits, axis=0)
            mass = jnp.sum(jnp.exp(logits - peak[None, :]), axis=0)
            return (
                lax.dynamic_update_slice_in_dim(top, peak, start, 0),
                lax.dynamic_update_slice_in_dim(total, mass, start, 0),
            )

        start_carry = (jnp.zeros((columns,), jnp.float32), jnp.zeros((columns,), jnp.float32))
        top, total = lax.fori_loop(0, count, column_visit, start_carry)
        top, total = merged_by_axis((top, total), ROW, lse_pair)
        return blur * jnp.log(1.0 / total_support) - blur * (top + jnp.log(total))

    dual_g = jnp.zeros((columns,), jnp.float32)
    dual_f = jnp.zeros((rows,), jnp.float32)
    for step in range(ITERS):
        dual_f = row_step(dual_g)
        dual_g = column_step(dual_f)

    def positions_visit(index, summed):
        start = index * width_block
        gpart = lax.dynamic_slice_in_dim(dual_g, start, width_block, 0)
        plan = jnp.exp((dual_f[:, None] + gpart[None, :] - tile_cost(start)) / blur)
        moved = jnp.dot(points_wide, plan, precision=lax.Precision.HIGHEST) * total_support
        return lax.dynamic_update_slice_in_dim(summed, moved, start, 1)

    terms = lax.fori_loop(0, count, positions_visit, jnp.zeros((dims, columns), jnp.float32))
    summed = total_of(terms, (("atlas", "row_0"), "row_1"))
    updated = summed / atlases
    return (dual_f[None, :], dual_g[None, :], updated)


def solution(mesh):
    split = Mesh(
        mesh.devices.reshape(mesh.shape["atlas"], 16, 2, mesh.shape["col"]),
        ("atlas", "row_0", "row_1", "col"),
    )
    in_specs = (P("atlas", None, ROW), P(None, "col"))
    out_specs = (P("atlas", ROW), P("atlas", "col"), P(None, "col"))
    return jax.shard_map(
        shards, mesh=split, in_specs=in_specs, out_specs=out_specs, check_vma=False
    )
```

profile of v0, /device:TPU:1, one launch (start us, length us, event | category | flops | bytes accessed | tf_op | source)
XLA Modules:
  0.0 239.9 jit_solution(8145299425401548114)
XLA Ops:
  1.6 1.2 multiply_reduce_fusion
  2.8 6.2 %while.78 = (s32[]{:T(128)}, f32[512]{0:T(512)S(1)}, f32[512]{0:T(512)S(1)}, f32[512]{0:T(512)S(1)}, f32[4096]{0:T(1024)S(1)}, /*index=5*/bf16[64,4096]{1,0:T(8,...) while((s32[]{:T(128)}, f32[512]{0:T(512)S(1)}, ...), condition=%wide.region_5.0_spmd.clone, body=%wide.region_2.0_spmd.clone.sunk | while | flops 35916292 | bytes 2263222 | solution.py:159
  9.7 4.8 %all-to-all-start = ((f32[4,2,512]{2,1,0:T(2,128)}), f32[4,2,512]{2,1,0:T(2,128)S(1)}, u32[]{:S(2)}, u32[]{:S(2)}) async-start(f32[4,2,512]{2,1,0:T(2,128)} %broadcast_in_dim.88), calls=%async_computation | async-start | bytes 32768 | tf_op jit(solution)/shard_map/all_to_all | solution.py:16
  14.5 4.2 %all-to-all-done = f32[4,2,512]{2,1,0:T(2,128)S(1)} async-done(((f32[4,2,512]{2,1,0:T(2,128)}), f32[4,2,512]{2,1,0:T(2,128)S(1)}, u32[]{:S(2)}, u32[]{:S(2)}) %all-to-all-start) | async-done | bytes 16416 | tf_op jit(solution)/shard_map/all_to_all | solution.py:16
  19.0 10.2 %while.75 = (s32[]{:T(128)}, f32[4096]{0:T(1024)S(1)}, f32[4096]{0:T(1024)S(1)}, f32[512]{0:T(512)S(1)}, f32[512]{0:T(512)S(1)}, /*index=5*/f32[4096]{0:T(1024)S...) while((s32[]{:T(128)}, f32[4096]{0:T(1024)S(1)}, ...), condition=%wide.region_9.10_spmd, body=%wide.region_6.9_spmd.sunk | while | flops 35912708 | bytes 2252987 | solution.py:177
  29.2 31.8 %all-gather.4 = f32[16,2,4096]{2,1,0:T(2,128)S(1)} all-gather(f32[1,2,4096]{2,1,0:T(2,128)S(1)} %maximum_bitcast_fusion), channel_id=2, replica_groups=mesh['atlas'=4,'row_0'=16,'row_1'=2,'col'=4] {'row_0'}, dimensions={0}, use_global_device_ids=true | all-gather | bytes 557056 | tf_op jit(solution)/shard_map/all_gather | solution.py:57
  61.8 10.1 %all-gather.5 = f32[2,2,4096]{2,1,0:T(2,128)S(1)} all-gather(f32[1,2,4096]{2,1,0:T(2,128)S(1)} %maximum_bitcast_fusion.1), channel_id=3, replica_groups=mesh['atlas'=4,'row_0'=16,'row_1'=2,'col'=4] {'row_1'}, dimensions={0}, use_global_device_ids=true | all-gather | bytes 98304 | tf_op jit(solution)/shard_map/all_gather | solution.py:57
  72.0 6.9 %while.79 = (s32[]{:T(128)}, f32[512]{0:T(512)S(1)}, f32[512]{0:T(512)S(1)}, f32[4096]{0:T(1024)S(1)}, f32[512]{0:T(512)S(1)}, /*index=5*/f32[4096]{0:T(1024)S(1...) while((s32[]{:T(128)}, f32[512]{0:T(512)S(1)}, ...), condition=%wide.region_13.14_spmd.clone, body=%wide.region_10.13_spmd.clone.sunk | while | flops 35916292 | bytes 2269378 | solution.py:159
  79.5 3.3 %all-to-all-start.1 = ((f32[4,2,512]{2,1,0:T(2,128)}), f32[4,2,512]{2,1,0:T(2,128)S(1)}, u32[]{:S(2)}, u32[]{:S(2)}) async-start(f32[4,2,512]{2,1,0:T(2,128)} %broadcast_in_dim.89), calls=%async_computation.1 | async-start | bytes 32768 | tf_op jit(solution)/shard_map/all_to_all | solution.py:16
  82.8 4.2 %all-to-all-done.1 = f32[4,2,512]{2,1,0:T(2,128)S(1)} async-done(((f32[4,2,512]{2,1,0:T(2,128)}), f32[4,2,512]{2,1,0:T(2,128)S(1)}, u32[]{:S(2)}, u32[]{:S(2)}) %all-to-all-start.1) | async-done | bytes 16416 | tf_op jit(solution)/shard_map/all_to_all | solution.py:16
  87.1 10.2 %while.76 = (s32[]{:T(128)}, f32[4096]{0:T(1024)S(1)}, f32[4096]{0:T(1024)S(1)}, f32[512]{0:T(512)S(1)}, f32[512]{0:T(512)S(1)}, /*index=5*/f32[4096]{0:T(1024)S...) while((s32[]{:T(128)}, f32[4096]{0:T(1024)S(1)}, ...), condition=%wide.region_17.18_spmd, body=%wide.region_14.17_spmd.sunk | while | flops 35912708 | bytes 2252987 | solution.py:177
  97.4 22.3 %all-gather.6 = f32[16,2,4096]{2,1,0:T(2,128)S(1)} all-gather(f32[1,2,4096]{2,1,0:T(2,128)S(1)} %maximum_bitcast_fusion.2), channel_id=4, replica_groups=mesh['atlas'=4,'row_0'=16,'row_1'=2,'col'=4] {'row_0'}, dimensions={0}, use_global_device_ids=true | all-gather | bytes 557056 | tf_op jit(solution)/shard_map/all_gather | solution.py:57
  120.6 9.9 %all-gather.7 = f32[2,2,4096]{2,1,0:T(2,128)S(1)} all-gather(f32[1,2,4096]{2,1,0:T(2,128)S(1)} %maximum_bitcast_fusion.3), channel_id=5, replica_groups=mesh['atlas'=4,'row_0'=16,'row_1'=2,'col'=4] {'row_1'}, dimensions={0}, use_global_device_ids=true | all-gather | bytes 98304 | tf_op jit(solution)/shard_map/all_gather | solution.py:57
  130.6 14.7 %while.77 = (s32[]{:T(128)}, f32[64,4096]{1,0:T(8,128)S(1)}, f32[512]{0:T(512)S(1)}, f32[4096]{0:T(1024)S(1)}, f32[512]{0:T(512)S(1)}, /*index=5*/f32[4096]{0:T(...) while((s32[]{:T(128)}, f32[64,4096]{1,0:T(8,128)S(1)}, ...), condition=%wide.region_19.20_spmd, body=%wide.region_18.19_spmd.sunk | while | flops 236748800 | bytes 2506947 | solution.py:194
  134.9 1.1 fusion.216
  136.8 1.1 fusion.216
  138.6 1.1 fusion.216
  140.4 1.1 fusion.216
  142.3 1.1 fusion.216
  146.8 4.5 %all_to_all.35 = f32[2,64,2048]{2,1,0:T(8,128)S(1)} all-to-all(f32[2,64,2048]{2,1,0:T(8,128)S(1)} %copy.11), channel_id=1, replica_groups=mesh['atlas'=4,'row_0'=16,'row_1'=2,'col'=4] {'row_1'}, dimensions={0} | all-to-all | bytes 2097152 | tf_op jit(solution)/shard_map/all_to_all | solution.py:100
  151.8 40.5 %all_to_all.37 = f32[64,1,2048]{2,1,0:T(1,128)S(1)} all-to-all(f32[64,1,2048]{2,1,0:T(1,128)S(1)} %all_to_all.25), channel_id=1, replica_groups=mesh['atlas'=4,'row_0'=16,'row_1'=2,'col'=4] {'atlas','row_0'}, dimensions={0} | all-to-all | bytes 1048576 | tf_op jit(solution)/shard_map/all_to_all | solution.py:108
  193.7 8.3 %all-to-all-start.4 = ((f32[64,1,2048]{2,1,0:T(1,128)}), f32[64,1,2048]{2,1,0:T(1,128)S(1)}, u32[]{:S(2)}, u32[]{:S(2)}) async-start(f32[64,1,2048]{2,1,0:T(1,128)} %broadcast_in_dim.91), calls=%async_computation.4 | async-start | bytes 1048576 | tf_op jit(solution)/shard_map/all_to_all | solution.py:16
  202.7 28.4 %all-to-all-done.4 = f32[64,1,2048]{2,1,0:T(1,128)S(1)} async-done(((f32[64,1,2048]{2,1,0:T(1,128)}), f32[64,1,2048]{2,1,0:T(1,128)S(1)}, u32[]{:S(2)}, u32[]{:S(2)}) %all-to-all-start.4) | async-done | bytes 524320 | tf_op jit(solution)/shard_map/all_to_all | solution.py:16
  231.4 7.3 %all_to_all.36 = f32[2,64,2048]{2,1,0:T(8,128)S(1)} all-to-all(f32[2,64,2048]{2,1,0:T(8,128)S(1)} %broadcast_in_dim.93), channel_id=1, replica_groups=mesh['atlas'=4,'row_0'=16,'row_1'=2,'col'=4] {'row_1'}, dimensions={0} | all-to-all | bytes 2097152 | tf_op jit(solution)/shard_map/all_to_all | solution.py:16
  (270 shorter events, 51.5 us)
Async XLA Ops:
  0.6 2.2 copy-start
  1.6 1.2 copy-start.1
  9.7 9.1 %all-to-all-start = ((f32[4,2,512]{2,1,0:T(2,128)}), f32[4,2,512]{2,1,0:T(2,128)S(1)}, u32[]{:S(2)}, u32[]{:S(2)}) async-start(f32[4,2,512]{2,1,0:T(2,128)} %broadcast_in_dim.88), calls=%async_computation | async-start | bytes 32768 | tf_op jit(solution)/shard_map/all_to_all | solution.py:16
  79.5 7.4 %all-to-all-start.1 = ((f32[4,2,512]{2,1,0:T(2,128)}), f32[4,2,512]{2,1,0:T(2,128)S(1)}, u32[]{:S(2)}, u32[]{:S(2)}) async-start(f32[4,2,512]{2,1,0:T(2,128)} %broadcast_in_dim.89), calls=%async_computation.1 | async-start | bytes 32768 | tf_op jit(solution)/shard_map/all_to_all | solution.py:16
  145.2 0.9 copy-start.2
  193.7 37.4 %all-to-all-start.4 = ((f32[64,1,2048]{2,1,0:T(1,128)}), f32[64,1,2048]{2,1,0:T(1,128)S(1)}, u32[]{:S(2)}, u32[]{:S(2)}) async-start(f32[64,1,2048]{2,1,0:T(1,128)} %broadcast_in_dim.91), calls=%async_computation.4 | async-start | bytes 1048576 | tf_op jit(solution)/shard_map/all_to_all | solution.py:16
where the time goes:
time: 240 us
  blocking collectives  126 us (52%)
  waiting for transfers between devices  36.8 us (15%)
  matrix products  27.8 us (12%)
  local copies, waits for them, and re-layouts  18.8 us (8%)
  starting transfers between devices  16.4 us (7%)
  other arithmetic  11.8 us (5%)
    all_gather x4, blocking collectives, gathered_once(): both, at, found = (lax.all_gather(jnp.concatenate(lines), axis), 0, {})  74 us
    all_to_all x1, blocking collectives, summed_rows(): lax.all_to_all(nearer, far, split_axis=0, concat_axis=0, tiled=True)  40.5 us
    all_to_all x3, waiting for transfers between devices, copy_for_each(): lax.all_to_all(jnp.broadcast_to(x[None], (length, *x.shape)), axis, 0, 0,...  36.8 us
    dot_general x40, matrix products, tile_cost(): lax.dot_general(points, piece, (((0,), (0,)), ((), ())), preferred_elemen...  18.6 us
    all_to_all x3, starting transfers between devices, copy_for_each(): lax.all_to_all(jnp.broadcast_to(x[None], (length, *x.shape)), axis, 0, 0,...  16.4 us
    dot_general x8, matrix products, positions_visit(): jnp.dot(points_wide, plan, precision=lax.Precision.HIGHEST) * total_support  9.18 us
    all_to_all x1, blocking collectives, copy_for_each(): lax.all_to_all(jnp.broadcast_to(x[None], (length, *x.shape)), axis, 0, 0,...  7.33 us
  transfers between devices with their start and end apart: 3, of which 3 were waited for; matrix products, arithmetic and copies ran while one was open for 0% of the time, Pallas kernels for 0%

commit v1 on v0

v1 whole, which is shorter than its diff:
```python
import functools
import math

import jax
import jax.numpy as jnp
from jax import lax
from jax.experimental import pallas as pl
from jax.experimental.pallas import tpu as pltpu
from jax.sharding import Mesh
from jax.sharding import PartitionSpec as P

ITERS = 2
BLUR = 0.1
AXES = ("atlas", "row_0", "row_1", "col")
F32, BF16 = jnp.float32, jnp.bfloat16
LOW = -1e30
DEPTH = 128
GUARD = 16


def remote(src, dst, send, recv, device):
    return pltpu.make_async_remote_copy(
        src_ref=src,
        dst_ref=dst,
        send_sem=send,
        recv_sem=recv,
        device_id=device,
        device_id_type=pl.DeviceIdType.MESH,
    )


def three_rows(v, rows):
    hi = v.astype(BF16).astype(F32)
    rest = v - hi
    mid = rest.astype(BF16).astype(F32)
    low = rest - mid
    i = lax.broadcasted_iota(jnp.int32, (rows, v.shape[1]), 0)
    return jnp.where(i == 0, hi, jnp.where(i == 1, mid, jnp.where(i == 2, low, 0.0)))


def kernel(sizes, total_cells, total_support, *refs):
    (
        cells, support, out_f, out_g, out_n,
        xt_f, xt_g, yc, yf, half_y, gbuf, xt_all, xc_all, ycut,
        fx, gpart, gpair, gz, bfull, av, usend, urecv, tsend, ty, g2,
        f_s, f_r, gp_s, gp_r, gz_s, gz_r, gb_s, gb_r, av_s, av_r,
        ring_s, ring_r, u_s, u_r, ty_s, ty_r, g2_s, g2_r, g2p_s, g2p_r,
        nz_s, nz_r, ny_s, ny_r, np_s, np_r,
    ) = refs
    NY, NZ, NC, NX = sizes
    my, mz, mc, mx = (lax.axis_index(a) for a in AXES)
    dims, rows = cells.shape[1:]
    columns = support.shape[1]
    half = columns // NC
    part = dims // NY
    unit = dims * BLUR / 2.0
    scale = math.log2(math.e) / unit
    log_cells = unit * math.log(1.0 / total_cells)
    log_support = unit * math.log(1.0 / total_support)
    other = 1 - mc

    def at_z(k):
        return (my, lax.rem(mz + k, NZ), mc, mx)

    def at_y(k):
        return (lax.rem(my + k, NY), mz, mc, mx)

    def at_x(k):
        return (my, mz, mc, lax.rem(mx + k, NX))

    pair = (my, mz, other, mx)

    def from_z(k):
        return lax.rem(mz + NZ - k, NZ)

    def far_first(i):
        return NZ // 2 + (1 - 2 * lax.rem(i, 2)) * ((i + 1) // 2)

    def each(count, visit):
        def body(i, carry):
            visit(i)
            return carry

        lax.fori_loop(0, count, body, 0)

    barrier = pltpu.get_barrier_semaphore()

    def greet(device):
        pl.semaphore_signal(barrier, inc=1, device_id=device, device_id_type=pl.DeviceIdType.MESH)

    each(NZ - 1, lambda i: greet(at_z(far_first(i))))
    for k in range(1, NX):
        greet(at_x(k))
    for k in range(1, NY):
        greet(at_y(k))
    greet(pair)

    x32 = cells[0].astype(F32)
    gbuf[mz] = x32
    half_x = 0.5 * jnp.sum(x32 * x32, axis=0, keepdims=True)
    lane = lax.broadcasted_iota(jnp.int32, (128, DEPTH), 1)
    ones_lane = jnp.where((lane >= dims) & (lane < dims + 3), 1.0, 0.0)
    spare = jnp.zeros((DEPTH - dims, 128), F32)

    def turned(block):
        return jnp.transpose(jnp.concatenate([block, spare], axis=0))

    for r in range(0, rows, 128):
        t = turned(x32[:, r : r + 128])
        xt_g[r : r + 128, :] = t.astype(BF16)
        xt_f[r : r + 128, :] = (t + ones_lane).astype(BF16)
    step = 512

    def prepare(i):
        at = pl.ds(pl.multiple_of(i * step, step), step)
        y = support[:, at]
        yc[0:dims, at] = y
        yf[0:dims, at] = y
        i16 = lax.broadcasted_iota(jnp.int32, (GUARD, step), 0)
        yc[dims : dims + GUARD, at] = jnp.where(i16 < 3, 1.0, 0.0).astype(BF16)
        zeros = jnp.zeros((DEPTH - dims - GUARD, step), BF16)
        yc[dims + GUARD : DEPTH, at] = zeros
        yf[dims + GUARD : DEPTH, at] = zeros
        y32 = y.astype(F32)
        squares = 0.5 * jnp.sum(y32 * y32, axis=0, keepdims=True)
        half_y[:, at] = squares
        yf[dims : dims + GUARD, at] = three_rows(-squares, GUARD).astype(BF16)

    each(columns // step, prepare)

    def put_a(ref, a):
        ref[:, dims : dims + 8] = jnp.transpose(three_rows(a, 8)).astype(BF16)

    eye = lax.broadcasted_iota(jnp.int32, (128, 128), 0) == lax.broadcasted_iota(jnp.int32, (128, 128), 1)
    wide = 1024
    tall = min(256, rows)

    def f_pass(slot):
        def visit(r):
            at = pl.ds(pl.multiple_of(r * tall, tall), tall)
            xt = xt_f[at, :]
            top = jnp.full((tall, 128), LOW, F32)
            total = jnp.zeros((tall, 128), F32)
            for c in range(0, columns, wide):
                logits = jnp.dot(xt, yf[:, c : c + wide], preferred_element_type=F32)
                tiles = [logits[:, k : k + 128] for k in range(0, wide, 128)]
                peak = functools.reduce(jnp.maximum, tiles, top)
                total = total * jnp.exp2((top - peak) * scale)
                for tile in tiles:
                    total = total + jnp.exp2((tile - peak) * scale)
                top = peak
            peak = jnp.max(top, axis=1, keepdims=True)
            total = jnp.sum(total * jnp.exp2((top - peak) * scale), axis=1, keepdims=True)
            lse = peak + unit * jnp.log(total)
            for k in range(tall // 128):
                piece = jnp.where(eye, lse[k * 128 : (k + 1) * 128], 0.0)
                row = jnp.sum(piece, axis=0, keepdims=True)
                slot[:, pl.ds(pl.multiple_of(r * tall + k * 128, 128), 128)] = row

        each(rows // tall, visit)

    def g_pass():
        high = min(256, rows)

        def visit(i):
            w = yc[:, pl.ds(pl.multiple_of(i * step, step), step)]
            top = jnp.full((8, step), LOW, F32)
            total = jnp.zeros((8, step), F32)
            for r in range(0, rows, high):
                logits = jnp.dot(xt_g[r : r + high, :], w, preferred_element_type=F32)
                logits = logits.reshape(high // 8, 8, step)
                peak = jnp.maximum(top, jnp.max(logits, axis=0))
                total = total * jnp.exp2((top - peak) * scale) + jnp.sum(
                    jnp.exp2((logits - peak[None]) * scale), axis=0
                )
                top = peak
            peak = jnp.max(top, axis=0, keepdims=True)
            total = jnp.sum(total * jnp.exp2((top - peak) * scale), axis=0, keepdims=True)
            lse = peak + unit * jnp.log(total)
            for k in range(step // 128):
                r = i * (step // 128) + k
                gpart[r // NZ, pl.ds(lax.rem(r, NZ), 1), :] = lse[:, k * 128 : (k + 1) * 128]

        each(columns // step, visit)

    def merged(pieces):
        peak = functools.reduce(jnp.maximum, pieces)
        total = sum(jnp.exp2((piece - peak) * scale) for piece in pieces)
        return peak + unit * jnp.log(total)

    ahead, behind = NZ // 2, NZ // 2 - 1

    def right(s):
        slot = gbuf.at[from_z(s)]
        return remote(slot, slot, ring_s.at[0, s], ring_r.at[0, s], at_z(1))

    def left(s):
        slot = gbuf.at[lax.rem(mz + s, NZ)]
        return remote(slot, slot, ring_s.at[1, s], ring_r.at[1, s], at_z(NZ - 1))

    def spread(slot):
        block = gbuf[slot]
        xc_all[slot, 0:dims, :] = block.astype(BF16)
        i16 = lax.broadcasted_iota(jnp.int32, (GUARD, rows), 0)
        xc_all[slot, dims : dims + GUARD, :] = jnp.where(i16 < 1, 1.0, 0.0).astype(BF16)
        for r in range(0, rows, 128):
            xt_all[slot, r : r + 128, :] = turned(block[:, r : r + 128]).astype(BF16)

    def ring_step(s):
        if 0 < s <= ahead:
            right(s - 1).wait_recv()
        if s < ahead:
            right(s).start()
        if 0 < s <= behind:
            left(s - 1).wait_recv()
        if s < behind:
            left(s).start()

    def ring_spread(s):
        if s == 0:
            spread(mz)
        if 0 < s <= ahead:
            spread(from_z(s))
        if 0 < s <= behind:
            spread(lax.rem(mz + s, NZ))

    turns = list(range(ahead + 1))

    def turn():
        if turns:
            s = turns.pop(0)
            ring_step(s)
            ring_spread(s - 1)

    f_pass(fx.at[0, mx])
    pl.semaphore_wait(barrier, NX + NZ + NY - 2)

    def f_copy(it, k):
        slot = fx.at[it, mx]
        return remote(slot, slot, f_s.at[it, k - 1], f_r.at[it, k - 1], at_x(k))

    def z_copy(k):
        slot = gz.at[mz]
        return remote(slot, slot, gz_s.at[k], gz_r.at[k], at_z(k))

    def a_copy(k):
        slot = av.at[mz]
        return remote(slot, slot, av_s.at[k], av_r.at[k], at_z(k))

    def g2_copy(k):
        slot = g2.at[mc, mz]
        return remote(slot, slot, g2_s.at[k], g2_r.at[k], at_z(k))

    gp_copy = remote(gpart.at[other], gpair, gp_s, gp_r, pair)
    gb_copy = remote(bfull.at[mc], bfull.at[mc], gb_s, gb_r, pair)

    def f_exchange(it):
        for k in range(1, NX):
            f_copy(it, k).start()
        if it == 0:
            turn()
        for k in range(1, NX):
            f_copy(it, k).wait_recv()
        return log_cells - merged([fx[it, k] for k in range(NX)])

    a = f_exchange(0)
    put_a(xt_g, a)
    g_pass()
    gp_copy.start()
    gp_copy.wait_recv()
    gz[mz] = merged([gpart[mc], gpair[...]])
    each(NZ - 1, lambda i: z_copy(far_first(i)).start())
    turn()
    turn()
    each(NZ - 1, lambda i: z_copy(i + 1).wait_recv())
    bfull[mc] = log_support - merged([gz[k] for k in range(NZ)])
    gb_copy.start()
    turn()
    gb_copy.wait_recv()
    for h in range(NC):
        for r in range(NZ):
            j = (h * NZ + r) * 128
            yf[dims : dims + GUARD, j : j + 128] = three_rows(bfull[h, r : r + 1], GUARD).astype(BF16)
    f_pass(fx.at[1, mx])
    a = f_exchange(1)
    av[mz] = a
    out_f[...] = (a + half_x) * (2.0 / dims)
    each(NZ - 1, lambda i: a_copy(far_first(i)).start())
    while turns:
        turn()
    ring_spread(ahead)
    first = pl.ds(pl.multiple_of(mz * 128, 128), 128)
    second = pl.ds(pl.multiple_of(half + mz * 128, 128), 128)
    ycut[0] = yc[:, first]
    ycut[1] = yc[:, second]
    each(NZ - 1, lambda i: a_copy(i + 1).wait_recv())
    each(NZ, lambda k: put_a(xt_all.at[k], av[k]))

    weights = jnp.concatenate([ycut[0], ycut[1]], axis=1)

    def weigh(k, carry):
        top, total = carry
        logits = jnp.dot(xt_all[k], weights, preferred_element_type=F32)
        peak = jnp.maximum(top, jnp.max(logits, axis=0, keepdims=True))
        plan = jnp.exp2((logits - peak) * scale)
        hi = plan.astype(BF16)
        low = (plan - hi.astype(F32)).astype(BF16)
        xc = xc_all[k]
        total = (
            total * jnp.exp2((top - peak) * scale)
            + jnp.dot(xc, hi, preferred_element_type=F32)
            + jnp.dot(xc, low, preferred_element_type=F32)
        )
        return peak, total

    lines = dims + GUARD
    top, total = lax.fori_loop(
        0, NZ, weigh, (jnp.full((1, 256), LOW, F32), jnp.zeros((lines, 256), F32))
    )
    for h in range(NC):
        usend[h, 0:lines, :] = total[:, h * 128 : (h + 1) * 128]
        usend[h, lines : lines + 8, :] = jnp.broadcast_to(top[:, h * 128 : (h + 1) * 128], (8, 128))
    u_copy = remote(usend.at[other], urecv, u_s, u_r, pair)
    u_copy.start()
    u_copy.wait_recv()
    mine, theirs = usend[mc], urecv[...]
    peak = jnp.maximum(mine[lines : lines + 1], theirs[lines : lines + 1])
    total = mine[0:lines] * jnp.exp2((mine[lines : lines + 1] - peak) * scale) + theirs[
        0:lines
    ] * jnp.exp2((theirs[lines : lines + 1] - peak) * scale)
    mass = total[dims : dims + 1]
    tsend[...] = total[0:dims] / mass

    def t_copy(k):
        at = pl.ds(pl.multiple_of(lax.rem(my + k, NY) * part, part), part)
        return remote(tsend.at[at], ty.at[my], ty_s.at[k - 1], ty_r.at[k - 1], at_y(k))

    for k in range(1, NY):
        t_copy(k).start()
    g2[mc, mz] = log_support - peak - unit * jnp.log(mass)
    each(NZ - 1, lambda i: g2_copy(far_first(i)).start())
    band = pl.ds(pl.multiple_of(my * part, part), part)
    ty[my] = tsend[band, :]
    for k in range(1, NY):
        t_copy(k).wait_recv()

    def place(z):
        return out_n.at[band, pl.ds(pl.multiple_of(mc * half + z * 128, 128), 128)]

    place(mz)[...] = sum(ty[k] for k in range(NY)) * (1.0 / NY)

    def n_copy(k):
        return remote(place(mz), place(mz), nz_s.at[k], nz_r.at[k], at_z(k))

    each(NZ - 1, lambda i: n_copy(far_first(i)).start())

    def forward(z):
        for k in range(1, NY):
            remote(place(z), place(z), ny_s.at[k - 1], ny_r.at[k - 1], at_y(k)).start()

    forward(mz)

    def arrived(i):
        k = far_first(NZ - 2 - i)
        n_copy(k).wait_recv()
        forward(from_z(k))

    each(NZ - 1, arrived)
    own_half = pl.ds(pl.multiple_of(mc * half, half), half)

    def strip(y):
        return out_n.at[pl.ds(pl.multiple_of(y * part, part), part), own_half]

    def np_copy(k):
        piece = strip(lax.rem(my + NY - k, NY))
        return remote(piece, piece, np_s.at[k], np_r.at[k], pair)

    np_copy(0).start()
    each(NZ - 1, lambda i: g2_copy(i + 1).wait_recv())
    g2p_copy = remote(g2.at[mc], g2.at[mc], g2p_s, g2p_r, pair)
    g2p_copy.start()

    def ny_whole(k):
        piece = strip(lax.rem(my + NY - k, NY))
        return remote(piece, piece, ny_s.at[k - 1], ny_r.at[k - 1], at_y(k))

    for k in range(1, NY):
        ny_whole(k).wait_recv()
        np_copy(k).start()
    g2p_copy.wait_recv()
    for h in range(NC):
        for r in range(NZ):
            at = slice((h * NZ + r) * 128, (h * NZ + r + 1) * 128)
            out_g[:, at] = (g2[h, r] + half_y[:, at]) * (2.0 / dims)
    for k in range(NY):
        np_copy(k).wait_recv()

    for it in range(ITERS):
        for k in range(1, NX):
            f_copy(it, k).wait_send()
    gp_copy.wait_send()
    gb_copy.wait_send()
    u_copy.wait_send()
    g2p_copy.wait_send()
    for k in range(1, NY):
        t_copy(k).wait_send()
        ny_whole(k).wait_send()
    for k in range(NY):
        np_copy(k).wait_send()
    for s in range(ahead):
        right(s).wait_send()
    for s in range(behind):
        left(s).wait_send()

    def left_z(i):
        for copy in (z_copy, a_copy, g2_copy, n_copy):
            copy(i + 1).wait_send()

    each(NZ - 1, left_z)


def solution(mesh):
    NY, NX = mesh.shape["atlas"], mesh.shape["col"]
    NC = 2
    NZ = mesh.shape["row"] // NC
    split = Mesh(mesh.devices.reshape(NY, NZ, NC, NX), AXES)
    dma = pltpu.SemaphoreType.DMA

    def shards(cells, support):
        dims, rows = cells.shape[1:]
        columns = support.shape[1]
        part = dims // NY
        lines = dims + GUARD
        vmem = pltpu.VMEM
        scratch = [
            vmem((rows, DEPTH), BF16),
            vmem((rows, DEPTH), BF16),
            vmem((DEPTH, columns), BF16),
            vmem((DEPTH, columns), BF16),
            vmem((1, columns), F32),
            vmem((NZ, dims, rows), F32),
            vmem((NZ, rows, DEPTH), BF16),
            vmem((NZ, lines, rows), BF16),
            vmem((NC, DEPTH, 128), BF16),
            vmem((ITERS, NX, 1, rows), F32),
            vmem((NC, NZ, 128), F32),
            vmem((NZ, 128), F32),
            vmem((NZ, NZ, 128), F32),
            vmem((NC, NZ, 128), F32),
            vmem((NZ, 1, rows), F32),
            vmem((NC, lines + 8, 128), F32),
            vmem((lines + 8, 128), F32),
            vmem((dims, 128), F32),
            vmem((NY, part, 128), F32),
            vmem((NC, NZ, 1, 128), F32),
            dma((ITERS, NX - 1)), dma((ITERS, NX - 1)),
            dma, dma,
            dma((NZ,)), dma((NZ,)),
            dma, dma,
            dma((NZ,)), dma((NZ,)),
            dma((2, NZ // 2)), dma((2, NZ // 2)),
            dma, dma,
            dma((NY - 1,)), dma((NY - 1,)),
            dma((NZ,)), dma((NZ,)),
            dma, dma,
            dma((NZ,)), dma((NZ,)),
            dma((NY - 1,)), dma((NY - 1,)),
            dma((NY,)), dma((NY,)),
        ]
        body = functools.partial(kernel, (NY, NZ, NC, NX), rows * NZ * NC, columns * NX)
        return pl.pallas_call(
            body,
            out_shape=(
                jax.ShapeDtypeStruct((1, rows), F32),
                jax.ShapeDtypeStruct((1, columns), F32),
                jax.ShapeDtypeStruct((dims, columns), F32),
            ),
            in_specs=[pl.BlockSpec(memory_space=pltpu.VMEM)] * 2,
            out_specs=[pl.BlockSpec(memory_space=pltpu.VMEM)] * 3,
            scratch_shapes=scratch,
            compiler_params=pltpu.CompilerParams(
                collective_id=0, has_side_effects=True, vmem_limit_bytes=56 << 20
            ),
        )(cells, support)

    row = ("row_0", "row_1")
    in_specs = (P("atlas", None, row), P(None, "col"))
    out_specs = (P("atlas", row), P("atlas", "col"), P(None, "col"))
    return jax.shard_map(shards, mesh=split, in_specs=in_specs, out_specs=out_specs, check_vma=False)
```

time: 240 us -> 111 us (0.46)
  blocking collectives: 126 us -> 0 us
  Pallas kernels: 0 us -> 105 us
  waiting for transfers between devices: 36.8 us -> 0 us
  matrix products: 27.8 us -> 0 us
  starting transfers between devices: 16.4 us -> 0 us
  local copies, waits for them, and re-layouts: 18.8 us -> 4.83 us
  other arithmetic: 11.8 us -> 0 us
    pallas_call x0 -> x1, Pallas kernels: none -> 105 us  [shards(): pl.pallas_call(body, out_shape=(jax.ShapeDtypeStruct((1, rows), F32), jax...]
    all_gather x4 -> x0, blocking collectives: 74 us -> none  [gathered_once(): both, at, found = (lax.all_gather(jnp.concatenate(lines), axis), 0, {})]
    all_to_all x3 -> x0, blocking collectives: 52.4 us -> none  [the longest x1 40.5 us: summed_rows(): lax.all_to_all(nearer, far, split_axis=0, concat_axis=0, tiled=True)]
    all_to_all x3 -> x0, waiting for transfers between devices: 36.8 us -> none  [copy_for_each(): lax.all_to_all(jnp.broadcast_to(x[None], (length, *x.shape)), axis, 0, 0,...]
    dot_general x48 -> x0, matrix products: 27.8 us -> none  [the longest x40 18.6 us: tile_cost(): lax.dot_general(points, piece, (((0,), (0,)), ((), ())), preferred_elemen...]
    all_to_all x3 -> x0, starting transfers between devices: 16.4 us -> none  [copy_for_each(): lax.all_to_all(jnp.broadcast_to(x[None], (length, *x.shape)), axis, 0, 0,...]
    reduce_sum x36 -> x0, other arithmetic: 8.82 us -> none  [the longest x16 3.14 us: row_visit(): jnp.sum(jnp.exp(logits - peak[:, None]), axis=1)]
    dynamic_update_slice x32 -> x0, local copies, waits for them, and re-layouts: 8.62 us -> none  [the longest x16 4.39 us: column_visit(): lax.dynamic_update_slice_in_dim(top, peak, start, 0)]
  transfers between devices with their start and end apart: 3 -> 0, of which waited for: 3 -> 0; matrix products, arithmetic and copies ran while one was open for 0% -> 0% of each run, Pallas kernels for 0% -> 0%
where the time goes in v1:
time: 111 us; the launch traced here: 110 us
  Pallas kernels  105 us (95%)
  local copies, waits for them, and re-layouts  4.83 us (4%)
    pallas_call x1, Pallas kernels, shards(): pl.pallas_call(body, out_shape=(jax.ShapeDtypeStruct((1, rows), F32), jax...  105 us
    unnamed x5, local copies, waits for them, and re-layouts  4.83 us

profile of v1, /device:TPU:1, one launch (start us, length us, event | category | flops | bytes accessed | tf_op | source)
XLA Modules:
  0.0 110.3 jit_solution(18261445659224102002)
XLA Ops:
  0.6 104.8 %shard_map.49 = (f32[1,512]{1,0:T(1,128)}, f32[1,4096]{1,0:T(1,128)}, f32[64,4096]{1,0:T(8,128)}) custom-call(bf16[1,64,512]{2,1,0:T(8,128)(2,1)} %refs_0_.1, bf16[64,4096]{1,0:T(8,128)(2,1)} %refs_1_.1), custom_call_target="tpu_custom_call" | custom-call | tf_op jit(solution)/shard_map/pallas_call | solution.py:471
  105.4 0.0 copy-start
  105.4 0.7 copy-done
  106.1 0.6 copy.8
  106.7 1.3 %copy.9 = f32[1,4096]{1,0:T(1,128)} copy(f32[1,4096]{1,0:T(1,128)} %get-tuple-element.7) | data formatting | bytes 32768
  108.0 2.3 %copy.10 = f32[64,4096]{1,0:T(8,128)} copy(f32[64,4096]{1,0:T(8,128)} %get-tuple-element.8) | data formatting | bytes 2097152
Async XLA Ops:
  105.4 0.7 copy-start

commit v2 on v1

--- a/solution.py
+++ b/solution.py
@@ -16,6 +16,8 @@
 LOW = -1e30
 DEPTH = 128
 GUARD = 16
+CHUNKS = 2
+GROUP = 4
 
 
 def remote(src, dst, send, recv, device):
@@ -41,7 +43,7 @@
 def kernel(sizes, total_cells, total_support, *refs):
     (
         cells, support, out_f, out_g, out_n,
-        xt_f, xt_g, yc, yf, half_y, gbuf, xt_all, xc_all, ycut,
+        xt_f, xt_g, yc, yf, half_y, gbuf, xg_all, y_own,
         fx, gpart, gpair, gz, bfull, av, usend, urecv, tsend, ty, g2,
         f_s, f_r, gp_s, gp_r, gz_s, gz_r, gb_s, gb_r, av_s, av_r,
         ring_s, ring_r, u_s, u_r, ty_s, ty_r, g2_s, g2_r, g2p_s, g2p_r,
@@ -110,6 +112,8 @@
         xt_g[r : r + 128, :] = t.astype(BF16)
         xt_f[r : r + 128, :] = (t + ones_lane).astype(BF16)
     step = 512
+    for p in range(NZ):
+        xg_all[p, dims + GUARD : DEPTH, :] = jnp.zeros((DEPTH - dims - GUARD, rows), BF16)
 
     def prepare(i):
         at = pl.ds(pl.multiple_of(i * step, step), step)
@@ -135,8 +139,9 @@
     wide = 1024
     tall = min(256, rows)
 
-    def f_pass(slot):
+    def f_pass(slot, first, last):
         def visit(r):
+            r = r + first
             at = pl.ds(pl.multiple_of(r * tall, tall), tall)
             xt = xt_f[at, :]
             top = jnp.full((tall, 128), LOW, F32)
@@ -157,12 +162,13 @@
                 row = jnp.sum(piece, axis=0, keepdims=True)
                 slot[:, pl.ds(pl.multiple_of(r * tall + k * 128, 128), 128)] = row
 
-        each(rows // tall, visit)
-
-    def g_pass():
+        each(last - first, visit)
+
+    def g_pass(first, last):
         high = min(256, rows)
 
         def visit(i):
+            i = i + first
             w = yc[:, pl.ds(pl.multiple_of(i * step, step), step)]
             top = jnp.full((8, step), LOW, F32)
             total = jnp.zeros((8, step), F32)
@@ -181,7 +187,7 @@
                 r = i * (step // 128) + k
                 gpart[r // NZ, pl.ds(lax.rem(r, NZ), 1), :] = lse[:, k * 128 : (k + 1) * 128]
 
-        each(columns // step, visit)
+        each(last - first, visit)
 
     def merged(pieces):
         peak = functools.reduce(jnp.maximum, pieces)
@@ -190,49 +196,47 @@
 
     ahead, behind = NZ // 2, NZ // 2 - 1
 
-    def right(s):
-        slot = gbuf.at[from_z(s)]
-        return remote(slot, slot, ring_s.at[0, s], ring_r.at[0, s], at_z(1))
-
-    def left(s):
-        slot = gbuf.at[lax.rem(mz + s, NZ)]
-        return remote(slot, slot, ring_s.at[1, s], ring_r.at[1, s], at_z(NZ - 1))
-
-    def spread(slot):
-        block = gbuf[slot]
-        xc_all[slot, 0:dims, :] = block.astype(BF16)
-        i16 = lax.broadcasted_iota(jnp.int32, (GUARD, rows), 0)
-        xc_all[slot, dims : dims + GUARD, :] = jnp.where(i16 < 1, 1.0, 0.0).astype(BF16)
-        for r in range(0, rows, 128):
-            xt_all[slot, r : r + 128, :] = turned(block[:, r : r + 128]).astype(BF16)
-
-    def ring_step(s):
-        if 0 < s <= ahead:
-            right(s - 1).wait_recv()
-        if s < ahead:
-            right(s).start()
-        if 0 < s <= behind:
-            left(s - 1).wait_recv()
-        if s < behind:
-            left(s).start()
-
-    def ring_spread(s):
-        if s == 0:
-            spread(mz)
-        if 0 < s <= ahead:
-            spread(from_z(s))
-        if 0 < s <= behind:
-            spread(lax.rem(mz + s, NZ))
-
-    turns = list(range(ahead + 1))
-
-    def turn():
-        if turns:
-            s = turns.pop(0)
-            ring_step(s)
-            ring_spread(s - 1)
-
-    f_pass(fx.at[0, mx])
+    piece_dims = dims // CHUNKS
+
+    def ring_copy(direction, source, s, h, device):
+        piece = gbuf.at[source, pl.ds(h * piece_dims, piece_dims)]
+        return remote(piece, piece, ring_s.at[direction, s, h], ring_r.at[direction, s, h], device)
+
+    def right(s, h):
+        return ring_copy(0, from_z(s), s, h, at_z(1))
+
+    def left(s, h):
+        return ring_copy(1, lax.rem(mz + s, NZ), s, h, at_z(NZ - 1))
+
+    def source_of(p):
+        s = (p + 1) // 2
+        return from_z(s) if p % 2 else lax.rem(mz + s, NZ)
+
+    def spread(p):
+        xg_all[p, 0:dims, :] = gbuf[source_of(p)].astype(BF16)
+
+    turns = [(s, h) for s in range(ahead + 1) for h in range(CHUNKS)]
+
+    def turn(count=1):
+        for _ in range(min(count, len(turns))):
+            s, h = turns.pop(0)
+            if 0 < s <= ahead:
+                right(s - 1, h).wait_recv()
+            if s < ahead:
+                right(s, h).start()
+            if 0 < s <= behind:
+                left(s - 1, h).wait_recv()
+            if s < behind:
+                left(s, h).start()
+            if h == CHUNKS - 1:
+                if s == 0:
+                    spread(0)
+                if 0 < s <= ahead:
+                    spread(2 * s - 1)
+                if 0 < s <= behind:
+                    spread(2 * s)
+
+    f_pass(fx.at[0, mx], 0, rows // tall)
     pl.semaphore_wait(barrier, NX + NZ + NY - 2)
 
     def f_copy(it, k):
@@ -257,78 +261,89 @@
     def f_exchange(it):
         for k in range(1, NX):
             f_copy(it, k).start()
-        if it == 0:
-            turn()
+        turn(2)
         for k in range(1, NX):
             f_copy(it, k).wait_recv()
         return log_cells - merged([fx[it, k] for k in range(NX)])
 
     a = f_exchange(0)
     put_a(xt_g, a)
-    g_pass()
+    count = columns // step
+    g_pass(0, count // 2)
+    turn()
+    g_pass(count // 2, count)
     gp_copy.start()
+    turn()
     gp_copy.wait_recv()
     gz[mz] = merged([gpart[mc], gpair[...]])
     each(NZ - 1, lambda i: z_copy(far_first(i)).start())
-    turn()
-    turn()
+    turn(5)
     each(NZ - 1, lambda i: z_copy(i + 1).wait_recv())
     bfull[mc] = log_support - merged([gz[k] for k in range(NZ)])
     gb_copy.start()
-    turn()
     gb_copy.wait_recv()
     for h in range(NC):
         for r in range(NZ):
             j = (h * NZ + r) * 128
             yf[dims : dims + GUARD, j : j + 128] = three_rows(bfull[h, r : r + 1], GUARD).astype(BF16)
-    f_pass(fx.at[1, mx])
+    turn()
+    f_pass(fx.at[1, mx], 0, 1)
+    turn()
+    f_pass(fx.at[1, mx], 1, rows // tall)
     a = f_exchange(1)
     av[mz] = a
     out_f[...] = (a + half_x) * (2.0 / dims)
     each(NZ - 1, lambda i: a_copy(far_first(i)).start())
-    while turns:
-        turn()
-    ring_spread(ahead)
-    first = pl.ds(pl.multiple_of(mz * 128, 128), 128)
-    second = pl.ds(pl.multiple_of(half + mz * 128, 128), 128)
-    ycut[0] = yc[:, first]
-    ycut[1] = yc[:, second]
+    for h in range(NC):
+        at = pl.ds(pl.multiple_of(h * half + mz * 128, 128), 128)
+        y_own[h * 128 : (h + 1) * 128, :] = jnp.transpose(yc[:, at].astype(F32)).astype(BF16)
+    turn(4)
     each(NZ - 1, lambda i: a_copy(i + 1).wait_recv())
-    each(NZ, lambda k: put_a(xt_all.at[k], av[k]))
-
-    weights = jnp.concatenate([ycut[0], ycut[1]], axis=1)
-
-    def weigh(k, carry):
+
+    def weigh(first, carry):
         top, total = carry
-        logits = jnp.dot(xt_all[k], weights, preferred_element_type=F32)
-        peak = jnp.maximum(top, jnp.max(logits, axis=0, keepdims=True))
-        plan = jnp.exp2((logits - peak) * scale)
-        hi = plan.astype(BF16)
-        low = (plan - hi.astype(F32)).astype(BF16)
-        xc = xc_all[k]
-        total = (
-            total * jnp.exp2((top - peak) * scale)
-            + jnp.dot(xc, hi, preferred_element_type=F32)
-            + jnp.dot(xc, low, preferred_element_type=F32)
-        )
+        weights = y_own[...]
+        products, blocks = [], []
+        for p in range(first, first + GROUP):
+            rows16 = three_rows(av[source_of(p)], GUARD)
+            i16 = lax.broadcasted_iota(jnp.int32, rows16.shape, 0)
+            xg_all[p, dims : dims + GUARD, :] = jnp.where(i16 == 3, 1.0, rows16).astype(BF16)
+            blocks.append(xg_all[p])
+            products.append(jnp.dot(weights, blocks[-1], preferred_element_type=F32))
+        tiles = [x[:, k : k + 128] for x in products for k in range(0, rows, 128)]
+        peak = jnp.max(functools.reduce(jnp.maximum, tiles), axis=1, keepdims=True)
+        peak = jnp.maximum(top, peak)
+        total = total * jnp.exp2((top - peak) * scale)
+        for logits, block in zip(products, blocks):
+            plan = jnp.exp2((logits - peak) * scale)
+            hi = plan.astype(BF16)
+            low = (plan - hi.astype(F32)).astype(BF16)
+            for half_plan in (hi, low):
+                total = total + lax.dot_general(
+                    half_plan, block, (((1,), (1,)), ((), ())), preferred_element_type=F32
+                )
         return peak, total
 
-    lines = dims + GUARD
-    top, total = lax.fori_loop(
-        0, NZ, weigh, (jnp.full((1, 256), LOW, F32), jnp.zeros((lines, 256), F32))
-    )
+    wide_j = NC * 128
+    carry = jnp.full((wide_j, 1), LOW, F32), jnp.zeros((wide_j, DEPTH), F32)
+    for first in range(0, NZ, GROUP):
+        while turns and turns[0][0] <= (first + GROUP) // 2:
+            turn()
+        carry = weigh(first, carry)
+    top, total = carry
+    row_mass, row_top, lines = dims + 3, dims + 4, dims + 8
+    lane_u = lax.broadcasted_iota(jnp.int32, (wide_j, DEPTH), 1)
+    total = jnp.where(lane_u == row_top, top, total)
     for h in range(NC):
-        usend[h, 0:lines, :] = total[:, h * 128 : (h + 1) * 128]
-        usend[h, lines : lines + 8, :] = jnp.broadcast_to(top[:, h * 128 : (h + 1) * 128], (8, 128))
+        usend[h] = jnp.transpose(total[h * 128 : (h + 1) * 128])[0:lines]
     u_copy = remote(usend.at[other], urecv, u_s, u_r, pair)
     u_copy.start()
     u_copy.wait_recv()
     mine, theirs = usend[mc], urecv[...]
-    peak = jnp.maximum(mine[lines : lines + 1], theirs[lines : lines + 1])
-    total = mine[0:lines] * jnp.exp2((mine[lines : lines + 1] - peak) * scale) + theirs[
-        0:lines
-    ] * jnp.exp2((theirs[lines : lines + 1] - peak) * scale)
-    mass = total[dims : dims + 1]
+    top_one, top_two = mine[row_top : row_top + 1], theirs[row_top : row_top + 1]
+    peak = jnp.maximum(top_one, top_two)
+    total = mine * jnp.exp2((top_one - peak) * scale) + theirs * jnp.exp2((top_two - peak) * scale)
+    mass = total[row_mass : row_mass + 1]
     tsend[...] = total[0:dims] / mass
 
     def t_copy(k):
@@ -407,16 +422,37 @@
         ny_whole(k).wait_send()
     for k in range(NY):
         np_copy(k).wait_send()
-    for s in range(ahead):
-        right(s).wait_send()
-    for s in range(behind):
-        left(s).wait_send()
+    for h in range(CHUNKS):
+        for s in range(ahead):
+            right(s, h).wait_send()
+        for s in range(behind):
+            left(s, h).wait_send()
 
     def left_z(i):
         for copy in (z_copy, a_copy, g2_copy, n_copy):
             copy(i + 1).wait_send()
 
     each(NZ - 1, left_z)
+
+
+def handed_on(*refs):
+    arrays, results, held, done = refs[:3], refs[3:6], refs[6:9], refs[9]
+    pieces = []
+    for array, hold, result in zip(arrays, held, results):
+        lines = array.shape[0]
+        for at in range(0, lines, 16):
+            piece = slice(at, min(at + 16, lines))
+            pieces.append((array.at[piece], hold.at[piece], result.at[piece]))
+    pieces = pieces[2:] + pieces[:2]
+    inward = [pltpu.make_async_copy(p[0], p[1], done.at[0, k]) for k, p in enumerate(pieces)]
+    outward = [pltpu.make_async_copy(p[1], p[2], done.at[1, k]) for k, p in enumerate(pieces)]
+    for copy in inward:
+        copy.start()
+    for before, after in zip(inward, outward):
+        before.wait()
+        after.start()
+    for copy in outward:
+        copy.wait()
 
 
 def solution(mesh):
@@ -430,7 +466,7 @@
         dims, rows = cells.shape[1:]
         columns = support.shape[1]
         part = dims // NY
-        lines = dims + GUARD
+        lines = dims + 8
         vmem = pltpu.VMEM
         scratch = [
             vmem((rows, DEPTH), BF16),
@@ -439,17 +475,16 @@
             vmem((DEPTH, columns), BF16),
             vmem((1, columns), F32),
             vmem((NZ, dims, rows), F32),
-            vmem((NZ, rows, DEPTH), BF16),
-            vmem((NZ, lines, rows), BF16),
-            vmem((NC, DEPTH, 128), BF16),
+            vmem((NZ, DEPTH, rows), BF16),
+            vmem((NC * 128, DEPTH), BF16),
             vmem((ITERS, NX, 1, rows), F32),
             vmem((NC, NZ, 128), F32),
             vmem((NZ, 128), F32),
             vmem((NZ, NZ, 128), F32),
             vmem((NC, NZ, 128), F32),
             vmem((NZ, 1, rows), F32),
-            vmem((NC, lines + 8, 128), F32),
-            vmem((lines + 8, 128), F32),
+            vmem((NC, lines, 128), F32),
+            vmem((lines, 128), F32),
             vmem((dims, 128), F32),
             vmem((NY, part, 128), F32),
             vmem((NC, NZ, 1, 128), F32),
@@ -458,7 +493,7 @@
             dma((NZ,)), dma((NZ,)),
             dma, dma,
             dma((NZ,)), dma((NZ,)),
-            dma((2, NZ // 2)), dma((2, NZ // 2)),
+            dma((2, NZ // 2, CHUNKS)), dma((2, NZ // 2, CHUNKS)),
             dma, dma,
             dma((NY - 1,)), dma((NY - 1,)),
             dma((NZ,)), dma((NZ,)),
@@ -468,13 +503,14 @@
             dma((NY,)), dma((NY,)),
         ]
         body = functools.partial(kernel, (NY, NZ, NC, NX), rows * NZ * NC, columns * NX)
-        return pl.pallas_call(
+        shapes = (
+            jax.ShapeDtypeStruct((1, rows), F32),
+            jax.ShapeDtypeStruct((1, columns), F32),
+            jax.ShapeDtypeStruct((dims, columns), F32),
+        )
+        found = pl.pallas_call(
             body,
-            out_shape=(
-                jax.ShapeDtypeStruct((1, rows), F32),
-                jax.ShapeDtypeStruct((1, columns), F32),
-                jax.ShapeDtypeStruct((dims, columns), F32),
-            ),
+            out_shape=shapes,
             in_specs=[pl.BlockSpec(memory_space=pltpu.VMEM)] * 2,
             out_specs=[pl.BlockSpec(memory_space=pltpu.VMEM)] * 3,
             scratch_shapes=scratch,
@@ -482,6 +518,13 @@
                 collective_id=0, has_side_effects=True, vmem_limit_bytes=56 << 20
             ),
         )(cells, support)
+        return pl.pallas_call(
+            handed_on,
+            out_shape=shapes,
+            in_specs=[pl.BlockSpec(memory_space=pl.ANY)] * 3,
+            out_specs=[pl.BlockSpec(memory_space=pl.ANY)] * 3,
+            scratch_shapes=[vmem(shape.shape, F32) for shape in shapes] + [dma((2, 2 + dims // 16))],
+        )(*found)
 
     row = ("row_0", "row_1")
     in_specs = (P("atlas", None, row), P(None, "col"))

time: 111 us -> 88.6 us (0.80)
  Pallas kernels: 105 us -> 87.8 us
  local copies, waits for them, and re-layouts: 4.83 us -> 0 us
    pallas_call x1 -> x2, Pallas kernels: 105 us -> 87.8 us  [the longest x1 85.8 us: shards(): pl.pallas_call(body, out_shape=shapes, in_specs=[pl.BlockSpec(memory_spac...]
    unnamed x5 -> x0, local copies, waits for them, and re-layouts: 4.83 us -> none
where the time goes in v2:
time: 88.6 us; the launch traced here: 88.5 us
  Pallas kernels  87.8 us (99%)
    pallas_call x1, Pallas kernels, shards(): pl.pallas_call(body, out_shape=shapes, in_specs=[pl.BlockSpec(memory_spac...  85.8 us
    pallas_call x1, Pallas kernels, shards(): pl.pallas_call(handed_on, out_shape=shapes, in_specs=[pl.BlockSpec(memory...  2.02 us

profile of v2, /device:TPU:1, one launch (start us, length us, event | category | flops | bytes accessed | tf_op | source)
XLA Modules:
  0.0 88.5 jit_solution(16833914425708924259)
XLA Ops:
  0.6 85.8 %shard_map.49 = (f32[1,512]{1,0:T(1,128)}, f32[1,4096]{1,0:T(1,128)}, f32[64,4096]{1,0:T(8,128)}) custom-call(bf16[1,64,512]{2,1,0:T(8,128)(2,1)} %refs_0_.1, bf16[64,4096]{1,0:T(8,128)(2,1)} %refs_1_.1), custom_call_target="tpu_custom_call" | custom-call | tf_op jit(solution)/shard_map/pallas_call | solution.py:511
  86.5 2.0 %shard_map.50 = (f32[1,512]{1,0:T(1,128)}, f32[1,4096]{1,0:T(1,128)}, f32[64,4096]{1,0:T(8,128)}) custom-call(f32[1,512]{1,0:T(1,128)} %get-tuple-element.6.refs_0_, f32[1,4096]{1,0:T(1,128)} %get-tuple-element.7.refs_1_, f32[64,4096]{1,0:T(8,128)} %get-tuple-element.8.refs_2_), custom_call_target="tpu_custom_call" | custom-call | tf_op jit(solution)/shard_map/pallas_call | solution.py:521

commit v3 on v2

--- a/solution.py
+++ b/solution.py
@@ -16,7 +16,10 @@
 LOW = -1e30
 DEPTH = 128
 GUARD = 16
+GZ = 6
+AV = 4
 CHUNKS = 2
+SHARERS = 2
 GROUP = 4
 
 
@@ -42,17 +45,17 @@
 
 def kernel(sizes, total_cells, total_support, *refs):
     (
-        cells, support, out_f, out_g, out_n,
+        cells_in, support_in, out_f, out_g, out_n, cells, support, in_sem,
         xt_f, xt_g, yc, yf, half_y, gbuf, xg_all, y_own,
         fx, gpart, gpair, gz, bfull, av, usend, urecv, tsend, ty, g2,
         f_s, f_r, gp_s, gp_r, gz_s, gz_r, gb_s, gb_r, av_s, av_r,
-        ring_s, ring_r, u_s, u_r, ty_s, ty_r, g2_s, g2_r, g2p_s, g2p_r,
+        ring_s, ring_r, share_s, share_r, u_s, u_r, ty_s, ty_r, g2_s, g2_r, g2p_s, g2p_r,
         nz_s, nz_r, ny_s, ny_r, np_s, np_r,
     ) = refs
     NY, NZ, NC, NX = sizes
     my, mz, mc, mx = (lax.axis_index(a) for a in AXES)
-    dims, rows = cells.shape[1:]
-    columns = support.shape[1]
+    dims, rows = cells_in.shape[1:]
+    columns = support_in.shape[1]
     half = columns // NC
     part = dims // NY
     unit = dims * BLUR / 2.0
@@ -90,6 +93,12 @@
     def greet(device):
         pl.semaphore_signal(barrier, inc=1, device_id=device, device_id_type=pl.DeviceIdType.MESH)
 
+    loads = [
+        pltpu.make_async_copy(cells_in, cells, in_sem.at[0]),
+        pltpu.make_async_copy(support_in, support, in_sem.at[1]),
+    ]
+    for load in loads:
+        load.start()
     each(NZ - 1, lambda i: greet(at_z(far_first(i))))
     for k in range(1, NX):
         greet(at_x(k))
@@ -97,6 +106,7 @@
         greet(at_y(k))
     greet(pair)
 
+    loads[0].wait()
     x32 = cells[0].astype(F32)
     gbuf[mz] = x32
     half_x = 0.5 * jnp.sum(x32 * x32, axis=0, keepdims=True)
@@ -130,6 +140,7 @@
         half_y[:, at] = squares
         yf[dims : dims + GUARD, at] = three_rows(-squares, GUARD).astype(BF16)
 
+    loads[1].wait()
     each(columns // step, prepare)
 
     def put_a(ref, a):
@@ -167,9 +178,8 @@
     def g_pass(first, last):
         high = min(256, rows)
 
-        def visit(i):
-            i = i + first
-            w = yc[:, pl.ds(pl.multiple_of(i * step, step), step)]
+        for i in range(first, last):
+            w = yc[:, i * step : (i + 1) * step]
             top = jnp.full((8, step), LOW, F32)
             total = jnp.zeros((8, step), F32)
             for r in range(0, rows, high):
@@ -185,9 +195,7 @@
             lse = peak + unit * jnp.log(total)
             for k in range(step // 128):
                 r = i * (step // 128) + k
-                gpart[r // NZ, pl.ds(lax.rem(r, NZ), 1), :] = lse[:, k * 128 : (k + 1) * 128]
-
-        each(last - first, visit)
+                gpart[r // NZ, r % NZ : r % NZ + 1, :] = lse[:, k * 128 : (k + 1) * 128]
 
     def merged(pieces):
         peak = functools.reduce(jnp.maximum, pieces)
@@ -196,10 +204,19 @@
 
     ahead, behind = NZ // 2, NZ // 2 - 1
 
-    piece_dims = dims // CHUNKS
+    piece_dims = dims // (CHUNKS * SHARERS)
+    odd = lax.rem(mx, 2)
+    sharers = [
+        (my, mz, mc, mx + 1 - 2 * odd),
+        (my, mz, mc, lax.rem(mx + NX - 1 + 2 * odd, NX)),
+    ]
+
+    def carried(source, h):
+        first = pl.multiple_of((h * SHARERS + odd) * piece_dims, piece_dims)
+        return gbuf.at[source, pl.ds(first, piece_dims)]
 
     def ring_copy(direction, source, s, h, device):
-        piece = gbuf.at[source, pl.ds(h * piece_dims, piece_dims)]
+        piece = carried(source, h)
         return remote(piece, piece, ring_s.at[direction, s, h], ring_r.at[direction, s, h], device)
 
     def right(s, h):
@@ -212,8 +229,19 @@
         s = (p + 1) // 2
         return from_z(s) if p % 2 else lax.rem(mz + s, NZ)
 
+    def share(p, h):
+        piece = carried(source_of(p), h)
+        return remote(piece, piece, share_s.at[h, p], share_r.at[h, p], sharers[h])
+
+    unspread = list(range(NZ))
+
     def spread(p):
-        xg_all[p, 0:dims, :] = gbuf[source_of(p)].astype(BF16)
+        if p in unspread:
+            unspread.remove(p)
+            if p:
+                for h in range(CHUNKS):
+                    share(p, h).wait_recv()
+            xg_all[p, 0:dims, :] = gbuf[source_of(p)].astype(BF16)
 
     turns = [(s, h) for s in range(ahead + 1) for h in range(CHUNKS)]
 
@@ -224,17 +252,18 @@
                 right(s - 1, h).wait_recv()
             if s < ahead:
                 right(s, h).start()
+            if 0 < s <= ahead:
+                share(2 * s - 1, h).start()
             if 0 < s <= behind:
                 left(s - 1, h).wait_recv()
             if s < behind:
                 left(s, h).start()
+            if 0 < s <= behind:
+                share(2 * s, h).start()
             if h == CHUNKS - 1:
-                if s == 0:
-                    spread(0)
-                if 0 < s <= ahead:
-                    spread(2 * s - 1)
-                if 0 < s <= behind:
-                    spread(2 * s)
+                for p in (2 * s - 5, 2 * s - 4):
+                    if p >= 0:
+                        spread(p)
 
     f_pass(fx.at[0, mx], 0, rows // tall)
     pl.semaphore_wait(barrier, NX + NZ + NY - 2)
@@ -269,15 +298,16 @@
     a = f_exchange(0)
     put_a(xt_g, a)
     count = columns // step
-    g_pass(0, count // 2)
-    turn()
-    g_pass(count // 2, count)
+    for first in range(0, count, 2):
+        g_pass(first, first + 2)
+        if first + 4 == count:
+            turn()
     gp_copy.start()
     turn()
     gp_copy.wait_recv()
     gz[mz] = merged([gpart[mc], gpair[...]])
     each(NZ - 1, lambda i: z_copy(far_first(i)).start())
-    turn(5)
+    turn(GZ)
     each(NZ - 1, lambda i: z_copy(i + 1).wait_recv())
     bfull[mc] = log_support - merged([gz[k] for k in range(NZ)])
     gb_copy.start()
@@ -297,7 +327,7 @@
     for h in range(NC):
         at = pl.ds(pl.multiple_of(h * half + mz * 128, 128), 128)
         y_own[h * 128 : (h + 1) * 128, :] = jnp.transpose(yc[:, at].astype(F32)).astype(BF16)
-    turn(4)
+    turn(AV)
     each(NZ - 1, lambda i: a_copy(i + 1).wait_recv())
 
     def weigh(first, carry):
@@ -329,6 +359,8 @@
     for first in range(0, NZ, GROUP):
         while turns and turns[0][0] <= (first + GROUP) // 2:
             turn()
+        for p in range(first, first + GROUP):
+            spread(p)
         carry = weigh(first, carry)
     top, total = carry
     row_mass, row_top, lines = dims + 3, dims + 4, dims + 8
@@ -375,6 +407,25 @@
 
     forward(mz)
 
+    for it in range(ITERS):
+        for k in range(1, NX):
+            f_copy(it, k).wait_send()
+    for copy in (gp_copy, gb_copy, u_copy):
+        copy.wait_send()
+    for h in range(CHUNKS):
+        for p in range(1, NZ):
+            share(p, h).wait_send()
+        for s in range(ahead):
+            right(s, h).wait_send()
+        for s in range(behind):
+            left(s, h).wait_send()
+
+    def left_early(i):
+        for copy in (z_copy, a_copy):
+            copy(i + 1).wait_send()
+
+    each(NZ - 1, left_early)
+
     def arrived(i):
         k = far_first(NZ - 2 - i)
         n_copy(k).wait_recv()
@@ -410,49 +461,18 @@
     for k in range(NY):
         np_copy(k).wait_recv()
 
-    for it in range(ITERS):
-        for k in range(1, NX):
-            f_copy(it, k).wait_send()
-    gp_copy.wait_send()
-    gb_copy.wait_send()
-    u_copy.wait_send()
-    g2p_copy.wait_send()
     for k in range(1, NY):
         t_copy(k).wait_send()
         ny_whole(k).wait_send()
     for k in range(NY):
         np_copy(k).wait_send()
-    for h in range(CHUNKS):
-        for s in range(ahead):
-            right(s, h).wait_send()
-        for s in range(behind):
-            left(s, h).wait_send()
+    g2p_copy.wait_send()
 
     def left_z(i):
-        for copy in (z_copy, a_copy, g2_copy, n_copy):
+        for copy in (g2_copy, n_copy):
             copy(i + 1).wait_send()
 
     each(NZ - 1, left_z)
-
-
-def handed_on(*refs):
-    arrays, results, held, done = refs[:3], refs[3:6], refs[6:9], refs[9]
-    pieces = []
-    for array, hold, result in zip(arrays, held, results):
-        lines = array.shape[0]
-        for at in range(0, lines, 16):
-            piece = slice(at, min(at + 16, lines))
-            pieces.append((array.at[piece], hold.at[piece], result.at[piece]))
-    pieces = pieces[2:] + pieces[:2]
-    inward = [pltpu.make_async_copy(p[0], p[1], done.at[0, k]) for k, p in enumerate(pieces)]
-    outward = [pltpu.make_async_copy(p[1], p[2], done.at[1, k]) for k, p in enumerate(pieces)]
-    for copy in inward:
-        copy.start()
-    for before, after in zip(inward, outward):
-        before.wait()
-        after.start()
-    for copy in outward:
-        copy.wait()
 
 
 def solution(mesh):
@@ -469,6 +489,9 @@
         lines = dims + 8
         vmem = pltpu.VMEM
         scratch = [
+            vmem((1, dims, rows), BF16),
+            vmem((dims, columns), BF16),
+            dma((2,)),
             vmem((rows, DEPTH), BF16),
             vmem((rows, DEPTH), BF16),
             vmem((DEPTH, columns), BF16),
@@ -494,6 +517,7 @@
             dma, dma,
             dma((NZ,)), dma((NZ,)),
             dma((2, NZ // 2, CHUNKS)), dma((2, NZ // 2, CHUNKS)),
+            dma((CHUNKS, NZ)), dma((CHUNKS, NZ)),
             dma, dma,
             dma((NY - 1,)), dma((NY - 1,)),
             dma((NZ,)), dma((NZ,)),
@@ -508,23 +532,16 @@
             jax.ShapeDtypeStruct((1, columns), F32),
             jax.ShapeDtypeStruct((dims, columns), F32),
         )
-        found = pl.pallas_call(
+        return pl.pallas_call(
             body,
-            out_shape=shapes,
-            in_specs=[pl.BlockSpec(memory_space=pltpu.VMEM)] * 2,
+            out_shape=[pltpu.VMEM(shape.shape, F32) for shape in shapes],
+            in_specs=[pl.BlockSpec(memory_space=pl.ANY)] * 2,
             out_specs=[pl.BlockSpec(memory_space=pltpu.VMEM)] * 3,
             scratch_shapes=scratch,
             compiler_params=pltpu.CompilerParams(
                 collective_id=0, has_side_effects=True, vmem_limit_bytes=56 << 20
             ),
         )(cells, support)
-        return pl.pallas_call(
-            handed_on,
-            out_shape=shapes,
-            in_specs=[pl.BlockSpec(memory_space=pl.ANY)] * 3,
-            out_specs=[pl.BlockSpec(memory_space=pl.ANY)] * 3,
-            scratch_shapes=[vmem(shape.shape, F32) for shape in shapes] + [dma((2, 2 + dims // 16))],
-        )(*found)
 
     row = ("row_0", "row_1")
     in_specs = (P("atlas", None, row), P(None, "col"))

time: 88.6 us -> 83.8 us (0.946)
  Pallas kernels: 87.8 us -> 80.8 us
  local copies, waits for them, and re-layouts: 0 us -> 2.15 us
    pallas_call x2 -> x1, Pallas kernels: 87.8 us -> 80.8 us  [shards(): pl.pallas_call(body, out_shape=[pltpu.VMEM(shape.shape, F32) for shape in...]
    unnamed x0 -> x3, local copies, waits for them, and re-layouts: none -> 2.15 us
where the time goes in v3:
time: 83.8 us; the launch traced here: 83.6 us
  Pallas kernels  80.8 us (96%)
  local copies, waits for them, and re-layouts  2.15 us (3%)
    pallas_call x1, Pallas kernels, shards(): pl.pallas_call(body, out_shape=[pltpu.VMEM(shape.shape, F32) for shape in...  80.8 us
    unnamed x3, local copies, waits for them, and re-layouts  2.15 us

profile of v3, /device:TPU:1, one launch (start us, length us, event | category | flops | bytes accessed | tf_op | source)
XLA Modules:
  0.0 83.6 jit_solution(1460721394848461829)
XLA Ops:
  0.6 80.8 %shard_map.49 = (f32[1,512]{1,0:T(1,128)S(1)}, f32[1,4096]{1,0:T(1,128)S(1)}, f32[64,4096]{1,0:T(8,128)S(1)}) custom-call(bf16[1,64,512]{2,1,0:T(8,128)(2,1)} %refs_0_.1, bf16[64,4096]{1,0:T(8,128)(2,1)} %refs_1_.1), custom_call_target="tpu_custom_call" | custom-call | tf_op jit(solution)/shard_map/pallas_call | solution.py:535
  81.5 0.6 copy.8
  82.0 0.6 copy.9
  82.7 1.0 %copy.10 = f32[64,4096]{1,0:T(8,128)} copy(f32[64,4096]{1,0:T(8,128)S(1)} %get-tuple-element.5) | data formatting | bytes 2097152

commit v4 on v3

--- a/solution.py
+++ b/solution.py
@@ -46,7 +46,7 @@
 def kernel(sizes, total_cells, total_support, *refs):
     (
         cells_in, support_in, out_f, out_g, out_n, cells, support, in_sem,
-        xt_f, xt_g, yc, yf, half_y, gbuf, xg_all, y_own,
+        xt_f, xt_g, yc, yf, half_y, gbuf, xg_all, y_own, plans,
         fx, gpart, gpair, gz, bfull, av, usend, urecv, tsend, ty, g2,
         f_s, f_r, gp_s, gp_r, gz_s, gz_r, gb_s, gb_r, av_s, av_r,
         ring_s, ring_r, share_s, share_r, u_s, u_r, ty_s, ty_r, g2_s, g2_r, g2p_s, g2p_r,
@@ -366,10 +366,11 @@
     row_mass, row_top, lines = dims + 3, dims + 4, dims + 8
     lane_u = lax.broadcasted_iota(jnp.int32, (wide_j, DEPTH), 1)
     total = jnp.where(lane_u == row_top, top, total)
-    for h in range(NC):
-        usend[h] = jnp.transpose(total[h * 128 : (h + 1) * 128])[0:lines]
+    plans[...] = total
+    usend[other] = jnp.transpose(plans[pl.ds(pl.multiple_of(other * 128, 128), 128), :])[0:lines]
     u_copy = remote(usend.at[other], urecv, u_s, u_r, pair)
     u_copy.start()
+    usend[mc] = jnp.transpose(plans[pl.ds(pl.multiple_of(mc * 128, 128), 128), :])[0:lines]
     u_copy.wait_recv()
     mine, theirs = usend[mc], urecv[...]
     top_one, top_two = mine[row_top : row_top + 1], theirs[row_top : row_top + 1]
@@ -473,6 +474,21 @@
             copy(i + 1).wait_send()
 
     each(NZ - 1, left_z)
+
+
+def handed_on(*refs):
+    arrays, results, done = refs[:3], refs[3:6], refs[6]
+    pieces = []
+    for array, result in zip(arrays, results):
+        lines = array.shape[0]
+        for at in range(0, lines, 16):
+            piece = slice(at, min(at + 16, lines))
+            pieces.append((array.at[piece], result.at[piece]))
+    copies = [pltpu.make_async_copy(*piece, done.at[k]) for k, piece in enumerate(pieces)]
+    for copy in copies:
+        copy.start()
+    for copy in copies:
+        copy.wait()
 
 
 def solution(mesh):
@@ -500,6 +516,7 @@
             vmem((NZ, dims, rows), F32),
             vmem((NZ, DEPTH, rows), BF16),
             vmem((NC * 128, DEPTH), BF16),
+            vmem((NC * 128, DEPTH), F32),
             vmem((ITERS, NX, 1, rows), F32),
             vmem((NC, NZ, 128), F32),
             vmem((NZ, 128), F32),
@@ -532,7 +549,7 @@
             jax.ShapeDtypeStruct((1, columns), F32),
             jax.ShapeDtypeStruct((dims, columns), F32),
         )
-        return pl.pallas_call(
+        found = pl.pallas_call(
             body,
             out_shape=[pltpu.VMEM(shape.shape, F32) for shape in shapes],
             in_specs=[pl.BlockSpec(memory_space=pl.ANY)] * 2,
@@ -542,6 +559,14 @@
                 collective_id=0, has_side_effects=True, vmem_limit_bytes=56 << 20
             ),
         )(cells, support)
+        return pl.pallas_call(
+            handed_on,
+            out_shape=shapes,
+            in_specs=[pl.BlockSpec(memory_space=pl.ANY)] * 3,
+            out_specs=[pl.BlockSpec(memory_space=pl.ANY)] * 3,
+            scratch_shapes=[dma((2 + dims // 16,))],
+            compiler_params=pltpu.CompilerParams(vmem_limit_bytes=1 << 20),
+        )(*found)
 
     row = ("row_0", "row_1")
     in_specs = (P("atlas", None, row), P(None, "col"))

time: 83.8 us -> 82.6 us (0.986)
  local copies, waits for them, and re-layouts: 2.15 us -> 0 us
  Pallas kernels: 80.8 us -> 81.8 us
    unnamed x3 -> x0, local copies, waits for them, and re-layouts: 2.15 us -> none
    pallas_call x0 -> x1, Pallas kernels: none -> 1.03 us  [shards(): pl.pallas_call(handed_on, out_shape=shapes, in_specs=[pl.BlockSpec(memory...]
where the time goes in v4:
time: 82.6 us; the launch traced here: 82.4 us
  Pallas kernels  81.8 us (99%)
    pallas_call x1, Pallas kernels, shards(): pl.pallas_call(body, out_shape=[pltpu.VMEM(shape.shape, F32) for shape in...  80.8 us

profile of v4, /device:TPU:1, one launch (start us, length us, event | category | flops | bytes accessed | tf_op | source)
XLA Modules:
  0.0 82.4 jit_solution(12666300006985106562)
XLA Ops:
  0.6 80.8 %shard_map.49 = (f32[1,512]{1,0:T(1,128)S(1)}, f32[1,4096]{1,0:T(1,128)S(1)}, f32[64,4096]{1,0:T(8,128)S(1)}) custom-call(bf16[1,64,512]{2,1,0:T(8,128)(2,1)} %refs_0_.1, bf16[64,4096]{1,0:T(8,128)(2,1)} %refs_1_.1), custom_call_target="tpu_custom_call" | custom-call | tf_op jit(solution)/shard_map/pallas_call | solution.py:552
  81.4 1.0 %shard_map.50 = (f32[1,512]{1,0:T(1,128)}, f32[1,4096]{1,0:T(1,128)}, f32[64,4096]{1,0:T(8,128)}) custom-call(f32[1,512]{1,0:T(1,128)S(1)} %get-tuple-element.6.refs_0_, f32[1,4096]{1,0:T(1,128)S(1)} %get-tuple-element.7.refs_1_, f32[64,4096]{1,0:T(8,128)S(1)} %get-tuple-element.8.refs_2_), custom_call_target="tpu_custom_call" | custom-call | tf_op jit(solution)/shard_map/pallas_call | solution.py:562
